TPU v7x, 32 devices: a whole 2x2x4 slice. The times are simulated.
32 devices in a mesh: memory: 4 (over z), group: 8 (over y, x, core).
Axes of the slice: x: 2, y: 2, z: 4, core: 2. Of those that a mesh axis runs over, the one named last changes fastest.
Arguments:
- queries: bfloat16 [8, 32, 32, 128], P('group', 'memory')
- positives: bfloat16 [8, 32, 128, 128], P('group', 'memory'), may hold values from -6 to 6
- memory: bfloat16 [8, 512, 128, 128], P('group', 'memory'), may hold values from -6 to 6
- candidates: int32 [8, 32, 64], P('group', 'memory'), may hold values from 0 to 511, as said below
- counts: int32 [8, 32], P('group', 'memory'), may hold values from 16 to 32
Outputs:
- batch_scores: float32 [8, 32, 64], P('group', 'memory')
- memory_scores: float32 [8, 32, 64], P('group', 'memory')
- loss: float32 [8, 32], P('group', 'memory')
Inputs may be any that keep to these rules, and one draw needn't show every extreme that they name: `candidates`: passage id r of a column lies on memory index r // 128. Among the valid slots of the queries of one device (queries[g, m * 8 to (m + 1) * 8 - 1]), at most 96 name passages of any one memory index, and some memory index is named by exactly 96 of them. Ids may repeat.
All inputs are finite; a program needn't handle non-finite values.
Results may differ from a plain program's by a relative error of at most 0.0003.
Values may be sent and summed in bfloat16 or wider, within the bound.
No kernel may reach another device: no remote copies, remote signals or barrier semaphores. Data moves between devices by JAX's collectives and lax.ppermute only.
A program may use at most 128 MiB of HBM per device.

v0:
```python
import functools

import jax
import jax.numpy as jnp
from jax import lax
from jax.experimental import pallas as pl
from jax.experimental.pallas import tpu as pltpu
from jax.sharding import PartitionSpec as P

LANES = 128
MIB = 1024 * 1024
SLOTS = 8
CHUNK = 32
LIST_ROWS = 16


def token_max(passages, tokens):
    count, width, depth = passages.shape
    product = lax.dot_general(
        passages.reshape(count * width, depth),
        tokens,
        (((1,), (1,)), ((), ())),
        preferred_element_type=jnp.float32,
    )
    return jnp.max(product.reshape(count, width, tokens.shape[0]), axis=1)


def token_sum(best, queries):
    tokens = best.shape[1]
    per_query = tokens // queries
    row = lax.broadcasted_iota(jnp.int32, (queries, tokens), 0)
    col = lax.broadcasted_iota(jnp.int32, (queries, tokens), 1)
    own = (col // per_query == row).astype(jnp.float32)
    return lax.dot_general(
        own,
        best,
        (((1,), (1,)), ((), ())),
        precision=lax.Precision.HIGHEST,
        preferred_element_type=jnp.float32,
    )


def column_of(row):
    size = row.shape[1]
    square = (size, size)
    diagonal = lax.broadcasted_iota(jnp.int32, square, 0) == lax.broadcasted_iota(
        jnp.int32, square, 1
    )
    return jnp.sum(jnp.where(diagonal, jnp.broadcast_to(row, square), 0), axis=1, keepdims=True)


def row_of(column):
    size = column.shape[0]
    square = (size, size)
    diagonal = lax.broadcasted_iota(jnp.int32, square, 0) == lax.broadcasted_iota(
        jnp.int32, square, 1
    )
    return jnp.sum(jnp.where(diagonal, jnp.broadcast_to(column, square), 0), axis=0, keepdims=True)


def pack_kernel(p_count, query_ref, candidate_ref, count_ref, out_ref):
    _, q_count, slots = candidate_ref.shape
    _, _, q_tokens, depth = query_ref.shape
    out_ref[0, :q_count] = query_ref[0]
    ids = candidate_ref[0]
    row = lax.broadcasted_iota(jnp.int32, ids.shape, 0)
    valid_count = jnp.zeros(ids.shape, jnp.int32)
    for index in range(q_count):
        valid_count = jnp.where(row == index, count_ref[0, index], valid_count)
    valid = lax.broadcasted_iota(jnp.int32, ids.shape, 1) < valid_count
    holder = jnp.where(valid, ids // p_count, -1)
    planes = jnp.concatenate([ids % p_count, holder], axis=0).astype(jnp.float32)
    planes = jnp.concatenate(
        [planes, jnp.zeros((2 * q_count, depth - slots), jnp.float32)], axis=1
    )
    rest = jnp.zeros((q_tokens - 2 * q_count, depth), jnp.float32)
    out_ref[0, q_count] = jnp.concatenate([planes, rest], axis=0).astype(out_ref.dtype)


def pack(queries, candidates, counts, p_count):
    _, q_count, q_tokens, depth = queries.shape
    vmem = pl.BlockSpec(memory_space=pltpu.VMEM)
    return pl.pallas_call(
        functools.partial(pack_kernel, p_count),
        in_specs=[vmem, vmem, pl.BlockSpec(memory_space=pltpu.SMEM)],
        out_shape=jax.ShapeDtypeStruct((1, q_count + 1, q_tokens, depth), queries.dtype),
        compiler_params=pltpu.CompilerParams(vmem_limit_bytes=4 * MIB),
        name="pack",
    )(queries, candidates, counts)


def memory_kernel(shards, slots, *refs):
    packed_refs, memory_ref = refs[:shards], refs[shards]
    out_refs = refs[shards + 1 : 2 * shards + 1]
    passage_ref, query_ref, rank_ref, best_ref, list_ref, scalar_ref, copy_sems, list_sem = refs[
        2 * shards + 1 :
    ]
    q_count = out_refs[0].shape[0]
    p_count = passage_ref.shape[0]
    total = shards * q_count
    chunks = p_count // CHUNK

    def fetch(chunk):
        rows = pl.ds(pl.multiple_of(chunk * CHUNK, CHUNK), CHUNK)
        return pltpu.make_async_copy(
            memory_ref.at[0, rows], passage_ref.at[rows], copy_sems.at[chunk]
        )

    for chunk in range(chunks):
        fetch(chunk).start()

    me = lax.axis_index("memory").astype(jnp.float32)
    keys = []
    for index, packed_ref in enumerate(packed_refs):
        query_ref[index * q_count : (index + 1) * q_count] = packed_ref[0, :q_count]
        planes = packed_ref[0, q_count].astype(jnp.float32)
        local, holder = planes[:q_count], planes[q_count : 2 * q_count]
        keys.append(jnp.where(holder == me, local, -1.0))
    keys = jnp.concatenate(keys, axis=0)
    passage = lax.broadcasted_iota(jnp.int32, (total, p_count), 1).astype(jnp.float32)
    named = jnp.zeros((total, p_count), jnp.float32)
    for slot in range(slots):
        named = jnp.where(keys[:, slot : slot + 1] == passage, 1.0, named)

    square = (total, total)
    earlier = lax.broadcasted_iota(jnp.int32, square, 1) < lax.broadcasted_iota(
        jnp.int32, square, 0
    )
    before = jnp.dot(earlier.astype(jnp.float32), named, preferred_element_type=jnp.float32)
    rank_ref[...] = jnp.where(named > 0.0, before, -1.0)
    counts = jnp.sum(named, axis=0, keepdims=True)
    most = jnp.broadcast_to(jnp.max(counts, axis=1, keepdims=True), counts.shape)
    rest = jnp.zeros((LIST_ROWS - SLOTS - 2, p_count), jnp.float32)

    def write_list(first):
        asker = lax.broadcasted_iota(jnp.int32, (total, p_count), 0).astype(jnp.float32)
        rank = rank_ref[...] - first
        rows = [
            jnp.sum(jnp.where(rank == float(slot), asker, 0.0), axis=0, keepdims=True)
            for slot in range(SLOTS)
        ]
        list_ref[...] = jnp.concatenate(rows + [counts, most, rest], axis=0).astype(jnp.int32)
        copy = pltpu.make_async_copy(list_ref, scalar_ref, list_sem)
        copy.start()
        copy.wait()

    def unit(index):
        tokens = [query_ref[scalar_ref[slot, index]] for slot in range(SLOTS)]
        return token_max(passage_ref[pl.ds(index, 1)], jnp.concatenate(tokens, axis=0))

    def add_scores(first):
        sums = token_sum(best_ref[...], SLOTS)
        for index, out_ref in enumerate(out_refs):
            rank = rank_ref[index * q_count : (index + 1) * q_count] - first
            for slot in range(SLOTS):
                out_ref[...] = jnp.where(rank == float(slot), sums[slot : slot + 1], out_ref[...])

    for out_ref in out_refs:
        out_ref[...] = jnp.zeros_like(out_ref)
    write_list(0.0)

    @pl.loop(0, chunks)
    def _(chunk):
        fetch(chunk).wait()
        for start in range(0, CHUNK, 8):
            first = pl.multiple_of(chunk * CHUNK + start, 8)
            rows = [unit(first + offset) for offset in range(8)]
            best_ref[pl.ds(first, 8), :] = jnp.concatenate(rows, axis=0)

    add_scores(0.0)

    @pl.loop(1, (scalar_ref[SLOTS + 1, 0] + SLOTS - 1) // SLOTS)
    def _(turn):
        done = turn * SLOTS
        write_list(done.astype(jnp.float32))

        @pl.loop(0, p_count)
        def _(index):
            @pl.when(scalar_ref[SLOTS, index] > done)
            def _():
                best_ref[pl.ds(index, 1), :] = unit(index)

        add_scores(done.astype(jnp.float32))


def score_memory(packed, memory, slots):
    shards = len(packed)
    _, blocks, q_tokens, depth = packed[0].shape
    q_count = blocks - 1
    _, p_count, p_tokens, _ = memory.shape
    total = shards * q_count
    vmem = pl.BlockSpec(memory_space=pltpu.VMEM)
    return pl.pallas_call(
        functools.partial(memory_kernel, shards, slots),
        in_specs=[vmem] * shards + [pl.BlockSpec(memory_space=pltpu.HBM)],
        out_specs=[vmem] * shards,
        out_shape=[jax.ShapeDtypeStruct((q_count, p_count), jnp.float32)] * shards,
        scratch_shapes=[
            pltpu.VMEM((p_count, p_tokens, depth), memory.dtype),
            pltpu.VMEM((total, q_tokens, depth), memory.dtype),
            pltpu.VMEM((total, p_count), jnp.float32),
            pltpu.VMEM((p_count, SLOTS * q_tokens), jnp.float32),
            pltpu.VMEM((LIST_ROWS, p_count), jnp.int32),
            pltpu.SMEM((LIST_ROWS, p_count), jnp.int32),
            pltpu.SemaphoreType.DMA((p_count // CHUNK,)),
            pltpu.SemaphoreType.DMA,
        ],
        compiler_params=pltpu.CompilerParams(vmem_limit_bytes=57 * MIB),
        cost_estimate=pl.CostEstimate(
            flops=2 * SLOTS * q_tokens * p_count * p_tokens * depth,
            bytes_accessed=2 * p_count * p_tokens * depth,
            transcendentals=0,
        ),
        name="score_memory",
    )(*packed, memory)


def batch_kernel(chips, *refs):
    query_refs, passage_refs = refs[:2], refs[2 : 2 + chips]
    out_refs, best_ref = refs[2 + chips : 4 + chips], refs[4 + chips]
    _, queries, q_tokens, depth = query_refs[0].shape
    count = passage_refs[0].shape[1]
    if chips * count < best_ref.shape[0]:
        best_ref[...] = jnp.zeros_like(best_ref)
    for query_ref, out_ref in zip(query_refs, out_refs):
        tokens = query_ref[0].reshape(queries * q_tokens, depth)
        for chip, passage_ref in enumerate(passage_refs):
            best_ref[chip * count : (chip + 1) * count, :] = token_max(passage_ref[0], tokens)
        out_ref[...] = token_sum(best_ref[...], queries)


def score_batch(queries, mate_queries, positives):
    _, q_count, q_tokens, depth = queries.shape
    _, p_count, p_tokens, _ = positives[0].shape
    chips = len(positives)
    lanes = -(-chips * p_count // LANES) * LANES
    return pl.pallas_call(
        functools.partial(batch_kernel, chips),
        out_shape=[jax.ShapeDtypeStruct((q_count, lanes), jnp.float32)] * 2,
        scratch_shapes=[pltpu.VMEM((lanes, q_count * q_tokens), jnp.float32)],
        compiler_params=pltpu.CompilerParams(vmem_limit_bytes=16 * MIB),
        cost_estimate=pl.CostEstimate(
            flops=4 * chips * q_count * q_tokens * p_count * p_tokens * depth,
            bytes_accessed=2 * chips * p_count * p_tokens * depth,
            transcendentals=0,
        ),
        name="score_batch",
    )(queries, mate_queries, *positives)


def loss_kernel(shards, own_batch, mate_batch, *refs):
    memory_refs = refs[:shards]
    candidate_ref, count_ref, batch_ref, memory_ref, loss_ref = refs[shards:]
    group, shard = lax.axis_index("group"), lax.axis_index("memory")
    chip, core = group // 2, group % 2
    _, q_count, slots = candidate_ref.shape
    p_count = memory_refs[0].shape[1]
    columns = batch_ref.shape[2]

    parts = []
    for first in range(0, columns, LANES):
        lane = lax.broadcasted_iota(jnp.int32, (q_count, LANES), 1) + first
        owner = lane // q_count
        source = (((owner // 2) ^ chip) * q_count + lane % q_count) % LANES
        own = jnp.take_along_axis(own_batch[...], source, axis=1)
        mate = jnp.take_along_axis(mate_batch[...], source, axis=1)
        parts.append(jnp.where(owner % 2 == core, own, mate))
    batch = jnp.concatenate(parts, axis=1)[:, :columns]
    batch_ref[0] = batch

    ids = candidate_ref[0]
    padded = jnp.concatenate([ids, jnp.zeros((q_count, p_count - slots), jnp.int32)], axis=1)
    holder, local = padded // p_count, padded % p_count
    picked = jnp.zeros((q_count, p_count), jnp.float32)
    for step in range(shards):
        found = jnp.take_along_axis(memory_refs[step][...], local, axis=1)
        picked = jnp.where(holder == (shard ^ step), found, picked)

    valid = lax.broadcasted_iota(jnp.int32, (q_count, p_count), 1) < column_of(count_ref[...])
    memory_ref[0] = jnp.where(valid, picked, 0.0)[:, :slots]

    top = jnp.maximum(
        jnp.max(batch, axis=1, keepdims=True),
        jnp.max(jnp.where(valid, picked, -jnp.inf), axis=1, keepdims=True),
    )
    total = jnp.sum(jnp.exp(batch - top), axis=1, keepdims=True) + jnp.sum(
        jnp.where(valid, jnp.exp(picked - top), 0.0), axis=1, keepdims=True
    )
    column = lax.broadcasted_iota(jnp.int32, batch.shape, 1)
    own = group * q_count + lax.broadcasted_iota(jnp.int32, batch.shape, 0)
    target_score = jnp.sum(jnp.where(column == own, batch, 0.0), axis=1, keepdims=True)
    loss_ref[...] = row_of(top + jnp.log(total) - target_score)


def finish(own_batch, mate_batch, memory_parts, candidates, counts, columns):
    _, q_count, slots = candidates.shape
    return pl.pallas_call(
        functools.partial(loss_kernel, len(memory_parts)),
        out_shape=[
            jax.ShapeDtypeStruct((1, q_count, columns), jnp.float32),
            jax.ShapeDtypeStruct((1, q_count, slots), jnp.float32),
            jax.ShapeDtypeStruct((1, q_count), jnp.float32),
        ],
        compiler_params=pltpu.CompilerParams(vmem_limit_bytes=4 * MIB),
        name="finish",
    )(own_batch, mate_batch, *memory_parts, candidates, counts)


def body(queries, positives, memory, candidates, counts):
    shards = lax.axis_size("memory")
    groups = lax.axis_size("group")
    chips = groups // 2
    q_count = queries.shape[1]
    slots = candidates.shape[2] // 2

    def to_shard(array, step):
        return lax.ppermute(array, "memory", [(i, i ^ step) for i in range(shards)])

    def to_group(array, step):
        return lax.ppermute(array, "group", [(i, i ^ step) for i in range(groups)])

    own = pack(queries, candidates, counts, memory.shape[1])
    packed = [own] + [to_shard(own, step) for step in range(1, shards)]
    early, _ = lax.optimization_barrier((positives, own))
    late, late_queries, _ = lax.optimization_barrier((positives, queries, packed[1]))
    row = [positives]
    for step in range(1, chips):
        near = step & (step - 1) == 0
        row.append(to_group(early if near else late, 2 * step))
    mate_queries = to_group(late_queries, 1)

    scores = score_memory(packed, memory, slots)
    memory_parts = [scores[0]] + [to_shard(scores[step], step) for step in range(1, shards)]
    queries, mate_queries, _ = lax.optimization_barrier((queries, mate_queries, scores[0]))
    own_batch, mate_batch = score_batch(queries, mate_queries, row)
    mate_batch = to_group(mate_batch, 1)
    return finish(own_batch, mate_batch, memory_parts, candidates, counts, groups * q_count)


def solution(mesh):
    in_specs = (
        P("group", "memory", None, None),
        P("group", "memory", None, None),
        P("group", "memory", None, None),
        P("group", "memory", None),
        P("group", "memory"),
    )
    out_specs = (P("group", "memory", None), P("group", "memory", None), P("group", "memory"))
    return jax.shard_map(body, mesh=mesh, in_specs=in_specs, out_specs=out_specs, check_vma=False)
```

profile of v0, /device:TPU:0, one launch (start us, length us, event | category | flops | bytes accessed | tf_op | source)
XLA Modules:
  0.0 36.8 jit_solution(1544442318074658097)
XLA Ops:
  0.6 0.7 %copy-done.1 = s32[1,8,64]{2,1,0:T(8,128)S(1)} copy-done((s32[1,8,64]{2,1,0:T(8,128)S(1)}, s32[1,8,64]{2,1,0:T(8,128)}, u32[]{:S(2)}) %copy-start.1) | copy-done | bytes 2072
  1.3 0.7 %copy-done.4 = s32[1,8]{1,0:T(1,128)S(1)} copy-done((s32[1,8]{1,0:T(1,128)S(1)}, s32[1,8]{1,0:T(1,128)}, u32[]{:S(2)}) %copy-start.4) | copy-done | bytes 56
  2.0 0.9 %pack.1.refs_0_ = bf16[1,9,32,128]{3,2,1,0:T(8,128)(2,1)S(1)} custom-call(bf16[1,8,32,128]{3,2,1,0:T(8,128)(2,1)} %refs_0_, s32[1,8,64]{2,1,0:T(8,128)S(1)} %copy-done.1, s32[1,8]{1,0:T(1,128)S(1)} %copy-done.4), custom_call_target="tpu_custom_call" | custom-call | tf_op jit(solution)/shard_map/pack/pallas_call | solution.py:83
  2.9 3.1 %collective-permute-start = (bf16[1,9,32,128]{3,2,1,0:T(8,128)(2,1)S(1)}, bf16[1,9,32,128]{3,2,1,0:T(8,128)(2,1)S(1)}, u32[]{:S(2)}, u32[]{:S(2)}) collective-permute-start(bf16[1,9,32,128]{3,2,1,0:T(8,128)(2,1)S(1)} %pack.1.refs_0_), channel_id=1, source_target_pairs={{0,8},{8,0},{16,24},{24,16},{1,9},{9,1},{17,25},{25,17},{2,10},{10... | collective-permute-start | bytes 221192 | tf_op jit(solution)/shard_map/ppermute | solution.py:317
  6.0 1.5 %collective-permute-start.5 = (bf16[1,8,128,128]{3,2,1,0:T(8,128)(2,1)}, bf16[1,8,128,128]{3,2,1,0:T(8,128)(2,1)S(1)}, u32[]{:S(2)}, u32[]{:S(2)}) collective-permute-start(bf16[1,8,128,128]{3,2,1,0:T(8,128)(2,1)} %refs_2_.1), channel_id=1, source_target_pairs={{0,4},{1,5},{2,6},{3,7},{4,0},{5,1},{6,2},{7,3},{8,12},{9,13},{10,... | collective-permute-start | bytes 786440 | tf_op jit(solution)/shard_map/ppermute | solution.py:320
  7.5 1.5 %collective-permute-start.4 = (bf16[1,8,128,128]{3,2,1,0:T(8,128)(2,1)}, bf16[1,8,128,128]{3,2,1,0:T(8,128)(2,1)S(1)}, u32[]{:S(2)}, u32[]{:S(2)}) collective-permute-start(bf16[1,8,128,128]{3,2,1,0:T(8,128)(2,1)} %refs_2_.1), channel_id=1, source_target_pairs={{0,2},{1,3},{2,0},{3,1},{4,6},{5,7},{6,4},{7,5},{8,10},{9,11},{10,... | collective-permute-start | bytes 786440 | tf_op jit(solution)/shard_map/ppermute | solution.py:320
  9.0 0.0 collective-permute-done.refs_1_
  9.0 2.2 %collective-permute-start.6 = (bf16[1,8,128,128]{3,2,1,0:T(8,128)(2,1)}, bf16[1,8,128,128]{3,2,1,0:T(8,128)(2,1)S(1)}, u32[]{:S(2)}, u32[]{:S(2)}) collective-permute-start(bf16[1,8,128,128]{3,2,1,0:T(8,128)(2,1)} %refs_2_.1), channel_id=1, source_target_pairs={{0,6},{1,7},{2,4},{3,5},{4,2},{5,3},{6,0},{7,1},{8,14},{9,15},{10,... | collective-permute-start | bytes 786440 | tf_op jit(solution)/shard_map/ppermute | solution.py:320
  11.2 3.6 %collective-permute-start.3 = (bf16[1,9,32,128]{3,2,1,0:T(8,128)(2,1)S(1)}, bf16[1,9,32,128]{3,2,1,0:T(8,128)(2,1)S(1)}, u32[]{:S(2)}, u32[]{:S(2)}) collective-permute-start(bf16[1,9,32,128]{3,2,1,0:T(8,128)(2,1)S(1)} %pack.1.refs_0_), channel_id=1, source_target_pairs={{0,24},{8,16},{16,8},{24,0},{1,25},{9,17},{17,9},{25,1},{2,26},{10... | collective-permute-start | bytes 221192 | tf_op jit(solution)/shard_map/ppermute | solution.py:317
  14.8 0.0 collective-permute-start.2
  14.8 2.5 %collective-permute-done.3.refs_3_ = bf16[1,9,32,128]{3,2,1,0:T(8,128)(2,1)S(1)} collective-permute-done((bf16[1,9,32,128]{3,2,1,0:T(8,128)(2,1)S(1)}, bf16[1,9,32,128]{3,2,1,0:T(8,128)(2,1)S(1)}, u32[]{:S(2)}, u32[]{:S(2)}) %collective-permute-start.3) | collective-permute-done | bytes 73760 | tf_op jit(solution)/shard_map/ppermute | solution.py:317
  17.4 0.0 collective-permute-start.1
  17.4 2.8 %collective-permute-done.2.refs_2_ = bf16[1,9,32,128]{3,2,1,0:T(8,128)(2,1)S(1)} collective-permute-done((bf16[1,9,32,128]{3,2,1,0:T(8,128)(2,1)S(1)}, bf16[1,9,32,128]{3,2,1,0:T(8,128)(2,1)S(1)}, u32[]{:S(2)}, u32[]{:S(2)}) %collective-permute-start.2) | collective-permute-done | bytes 73760 | tf_op jit(solution)/shard_map/ppermute | solution.py:317
  20.2 0.0 copy-start.9
  20.2 0.6 %copy-done.9 = bf16[1,9,32,128]{3,2,1,0:T(8,128)(2,1)} copy-done((bf16[1,9,32,128]{3,2,1,0:T(8,128)(2,1)}, bf16[1,9,32,128]{3,2,1,0:T(8,128)(2,1)S(1)}, u32[]{:S(2)}) %copy-start.9) | copy-done | bytes 73752
  20.8 6.0 %score_memory.1 = (f32[8,128]{1,0:T(8,128)}, f32[8,128]{1,0:T(8,128)}, f32[8,128]{1,0:T(8,128)}, f32[8,128]{1,0:T(8,128)}) custom-call(bf16[1,9,32,128]{3,2,1,0:T(8,128)(2,1)} %copy-done, bf16[1,9,32,128]{3,2,1,0:T(8,128)(2,1)} %copy-done.7, bf16[1,9,32,128]{3,2,1,0:T(8,128)(2,1)} %copy-done.9, bf16[1,9,32,128]{3,2,1,0:T(8,128)(2,1)} %copy-done.8, ...), custom_call_target="tpu_custom_call" | custom-call | flops 1073741824 | bytes 4194304 | tf_op jit(solution)/shard_map/score_memory/pallas_call | solution.py:193
  26.8 0.1 collective-permute-start.8
  26.9 0.0 collective-permute-done.1.refs_1_
  26.9 2.7 %collective-permute-start.9 = (f32[8,128]{1,0:T(8,128)}, f32[8,128]{1,0:T(8,128)S(1)}, u32[]{:S(2)}, u32[]{:S(2)}) collective-permute-start(f32[8,128]{1,0:T(8,128)} %get-tuple-element.23), channel_id=1, source_target_pairs={{0,16},{8,24},{16,0},{24,8},{1,17},{9,25},{17,1},{25,9},{2,18},{10... | collective-permute-start | bytes 12296 | tf_op jit(solution)/shard_map/ppermute | solution.py:317
  29.6 0.0 collective-permute-done.5.refs_4_
  29.7 1.6 %collective-permute-start.10 = (f32[8,128]{1,0:T(8,128)}, f32[8,128]{1,0:T(8,128)S(1)}, u32[]{:S(2)}, u32[]{:S(2)}) collective-permute-start(f32[8,128]{1,0:T(8,128)} %get-tuple-element.24), channel_id=1, source_target_pairs={{0,24},{8,16},{16,8},{24,0},{1,25},{9,17},{17,9},{25,1},{2,26},{10... | collective-permute-start | bytes 12296 | tf_op jit(solution)/shard_map/ppermute | solution.py:317
  31.3 0.0 collective-permute-done.4.refs_3_
  31.3 0.0 collective-permute-done.6.refs_5_
  31.3 2.4 %score_batch.1 = (f32[8,128]{1,0:T(8,128)S(1)}, f32[8,128]{1,0:T(8,128)S(1)}) custom-call(bf16[1,8,32,128]{3,2,1,0:T(8,128)(2,1)} %refs_0_, bf16[1,8,32,128]{3,2,1,0:T(8,128)(2,1)S(1)} %collective-permute-done.1.refs_1_, bf16[1,8,128,128]{3,2,1,0:T(8,128)(2,1)S(1)} %copy-done.6, bf16[1,8,128,128]{3,2,1,0:T(8,128)(2,1)S(1)} %collective-permute-done.4.refs_3_, ...), custom_call_target="tpu_custom_call" | custom-call | flops 536870912 | bytes 1048576 | tf_op jit(solution)/shard_map/score_batch/pallas_call | solution.py:237
  33.7 0.0 collective-permute-start.7
  33.7 0.0 collective-permute-done.8.refs_1_
  33.7 0.0 collective-permute-done.9.refs_2_
  33.8 1.5 %collective-permute-done.10.refs_3_ = f32[8,128]{1,0:T(8,128)S(1)} collective-permute-done((f32[8,128]{1,0:T(8,128)}, f32[8,128]{1,0:T(8,128)S(1)}, u32[]{:S(2)}, u32[]{:S(2)}) %collective-permute-start.10) | collective-permute-done | bytes 4128 | tf_op jit(solution)/shard_map/ppermute | solution.py:317
  35.3 0.0 collective-permute-done.7.mate_batch
  35.3 0.0 copy-start.3
  35.3 0.7 %copy-done.3 = f32[8,128]{1,0:T(8,128)S(1)} copy-done((f32[8,128]{1,0:T(8,128)S(1)}, f32[8,128]{1,0:T(8,128)}, u32[]{:S(2)}) %copy-start.3) | copy-done | bytes 4120
  36.0 0.8 %finish.1 = (f32[1,8,64]{2,1,0:T(8,128)}, f32[1,8,64]{2,1,0:T(8,128)}, f32[1,8]{1,0:T(1,128)}) custom-call(f32[8,128]{1,0:T(8,128)S(1)} %get-tuple-element.20.own_batch, f32[8,128]{1,0:T(8,128)S(1)} %collective-permute-done.7.mate_batch, f32[8,128]{1,0:T(8,128)S(1)} %copy-done.3, f32[8,128]{1,0:T(8,128)S(1)} %collective-permute-done.8.refs_1_, ...), custom_call_target="tpu_custom_call" | custom-call | tf_op jit(solution)/shard_map/finish/pallas_call | solution.py:297
  (14 shorter events, 0.0 us)
Async XLA Ops:
  0.6 0.7 %copy-start.1 = (s32[1,8,64]{2,1,0:T(8,128)S(1)}, s32[1,8,64]{2,1,0:T(8,128)}, u32[]{:S(2)}) copy-start(s32[1,8,64]{2,1,0:T(8,128)} %refs_4_.3) | copy-start | bytes 6148
  1.3 0.7 %copy-start.4 = (s32[1,8]{1,0:T(1,128)S(1)}, s32[1,8]{1,0:T(1,128)}, u32[]{:S(2)}) copy-start(s32[1,8]{1,0:T(1,128)} %refs_5_.1) | copy-start | bytes 100
  2.0 29.3 %copy-start.6 = (bf16[1,8,128,128]{3,2,1,0:T(8,128)(2,1)S(1)}, bf16[1,8,128,128]{3,2,1,0:T(8,128)(2,1)}, u32[]{:S(2)}) copy-start(bf16[1,8,128,128]{3,2,1,0:T(8,128)(2,1)} %refs_2_.1) | copy-start | bytes 786436
  2.0 33.3 %copy-start.2 = (s32[1,8,64]{2,1,0:T(8,128)S(1)}, s32[1,8,64]{2,1,0:T(8,128)}, u32[]{:S(2)}) copy-start(s32[1,8,64]{2,1,0:T(8,128)} %refs_4_.3) | copy-start | bytes 6148
  2.0 33.3 %copy-start.5 = (s32[1,8]{1,0:T(1,128)S(1)}, s32[1,8]{1,0:T(1,128)}, u32[]{:S(2)}) copy-start(s32[1,8]{1,0:T(1,128)} %refs_5_.1) | copy-start | bytes 100
  2.9 17.3 %copy-start = (bf16[1,9,32,128]{3,2,1,0:T(8,128)(2,1)}, bf16[1,9,32,128]{3,2,1,0:T(8,128)(2,1)S(1)}, u32[]{:S(2)}) copy-start(bf16[1,9,32,128]{3,2,1,0:T(8,128)(2,1)S(1)} %pack.1.refs_0_) | copy-start | bytes 221188
  2.9 6.1 %collective-permute-start = (bf16[1,9,32,128]{3,2,1,0:T(8,128)(2,1)S(1)}, bf16[1,9,32,128]{3,2,1,0:T(8,128)(2,1)S(1)}, u32[]{:S(2)}, u32[]{:S(2)}) collective-permute-start(bf16[1,9,32,128]{3,2,1,0:T(8,128)(2,1)S(1)} %pack.1.refs_0_), channel_id=1, source_target_pairs={{0,8},{8,0},{16,24},{24,16},{1,9},{9,1},{17,25},{25,17},{2,10},{10... | collective-permute-start | bytes 221192 | tf_op jit(solution)/shard_map/ppermute | solution.py:317
  6.0 23.7 %collective-permute-start.5 = (bf16[1,8,128,128]{3,2,1,0:T(8,128)(2,1)}, bf16[1,8,128,128]{3,2,1,0:T(8,128)(2,1)S(1)}, u32[]{:S(2)}, u32[]{:S(2)}) collective-permute-start(bf16[1,8,128,128]{3,2,1,0:T(8,128)(2,1)} %refs_2_.1), channel_id=1, source_target_pairs={{0,4},{1,5},{2,6},{3,7},{4,0},{5,1},{6,2},{7,3},{8,12},{9,13},{10,... | collective-permute-start | bytes 786440 | tf_op jit(solution)/shard_map/ppermute | solution.py:320
  7.5 23.8 %collective-permute-start.4 = (bf16[1,8,128,128]{3,2,1,0:T(8,128)(2,1)}, bf16[1,8,128,128]{3,2,1,0:T(8,128)(2,1)S(1)}, u32[]{:S(2)}, u32[]{:S(2)}) collective-permute-start(bf16[1,8,128,128]{3,2,1,0:T(8,128)(2,1)} %refs_2_.1), channel_id=1, source_target_pairs={{0,2},{1,3},{2,0},{3,1},{4,6},{5,7},{6,4},{7,5},{8,10},{9,11},{10,... | collective-permute-start | bytes 786440 | tf_op jit(solution)/shard_map/ppermute | solution.py:320
  9.0 11.2 %copy-start.7 = (bf16[1,9,32,128]{3,2,1,0:T(8,128)(2,1)}, bf16[1,9,32,128]{3,2,1,0:T(8,128)(2,1)S(1)}, u32[]{:S(2)}) copy-start(bf16[1,9,32,128]{3,2,1,0:T(8,128)(2,1)S(1)} %collective-permute-done.refs_1_) | copy-start | bytes 221188
  9.0 22.3 %collective-permute-start.6 = (bf16[1,8,128,128]{3,2,1,0:T(8,128)(2,1)}, bf16[1,8,128,128]{3,2,1,0:T(8,128)(2,1)S(1)}, u32[]{:S(2)}, u32[]{:S(2)}) collective-permute-start(bf16[1,8,128,128]{3,2,1,0:T(8,128)(2,1)} %refs_2_.1), channel_id=1, source_target_pairs={{0,6},{1,7},{2,4},{3,5},{4,2},{5,3},{6,0},{7,1},{8,14},{9,15},{10,... | collective-permute-start | bytes 786440 | tf_op jit(solution)/shard_map/ppermute | solution.py:320
  11.2 6.2 %collective-permute-start.3 = (bf16[1,9,32,128]{3,2,1,0:T(8,128)(2,1)S(1)}, bf16[1,9,32,128]{3,2,1,0:T(8,128)(2,1)S(1)}, u32[]{:S(2)}, u32[]{:S(2)}) collective-permute-start(bf16[1,9,32,128]{3,2,1,0:T(8,128)(2,1)S(1)} %pack.1.refs_0_), channel_id=1, source_target_pairs={{0,24},{8,16},{16,8},{24,0},{1,25},{9,17},{17,9},{25,1},{2,26},{10... | collective-permute-start | bytes 221192 | tf_op jit(solution)/shard_map/ppermute | solution.py:317
  14.8 5.3 %collective-permute-start.2 = (bf16[1,9,32,128]{3,2,1,0:T(8,128)(2,1)S(1)}, bf16[1,9,32,128]{3,2,1,0:T(8,128)(2,1)S(1)}, u32[]{:S(2)}, u32[]{:S(2)}) collective-permute-start(bf16[1,9,32,128]{3,2,1,0:T(8,128)(2,1)S(1)} %pack.1.refs_0_), channel_id=1, source_target_pairs={{0,16},{8,24},{16,0},{24,8},{1,17},{9,25},{17,1},{25,9},{2,18},{10... | collective-permute-start | bytes 221192 | tf_op jit(solution)/shard_map/ppermute | solution.py:317
  17.4 2.8 %copy-start.8 = (bf16[1,9,32,128]{3,2,1,0:T(8,128)(2,1)}, bf16[1,9,32,128]{3,2,1,0:T(8,128)(2,1)S(1)}, u32[]{:S(2)}) copy-start(bf16[1,9,32,128]{3,2,1,0:T(8,128)(2,1)S(1)} %collective-permute-done.3.refs_3_) | copy-start | bytes 221188
  17.4 9.5 %collective-permute-start.1 = (bf16[1,8,32,128]{3,2,1,0:T(8,128)(2,1)}, bf16[1,8,32,128]{3,2,1,0:T(8,128)(2,1)S(1)}, u32[]{:S(2)}, u32[]{:S(2)}) collective-permute-start(bf16[1,8,32,128]{3,2,1,0:T(8,128)(2,1)} %refs_0_), channel_id=1, source_target_pairs={{0,1},{1,0},{2,3},{3,2},{4,5},{5,4},{6,7},{7,6},{8,9},{9,8},{10,11... | collective-permute-start | bytes 196616 | tf_op jit(solution)/shard_map/ppermute | solution.py:320
  20.2 0.6 %copy-start.9 = (bf16[1,9,32,128]{3,2,1,0:T(8,128)(2,1)}, bf16[1,9,32,128]{3,2,1,0:T(8,128)(2,1)S(1)}, u32[]{:S(2)}) copy-start(bf16[1,9,32,128]{3,2,1,0:T(8,128)(2,1)S(1)} %collective-permute-done.2.refs_2_) | copy-start | bytes 221188
  26.8 6.9 %collective-permute-start.8 = (f32[8,128]{1,0:T(8,128)}, f32[8,128]{1,0:T(8,128)S(1)}, u32[]{:S(2)}, u32[]{:S(2)}) collective-permute-start(f32[8,128]{1,0:T(8,128)} %get-tuple-element.22), channel_id=1, source_target_pairs={{0,8},{8,0},{16,24},{24,16},{1,9},{9,1},{17,25},{25,17},{2,10},{10... | collective-permute-start | bytes 12296 | tf_op jit(solution)/shard_map/ppermute | solution.py:317
  26.9 6.9 %collective-permute-start.9 = (f32[8,128]{1,0:T(8,128)}, f32[8,128]{1,0:T(8,128)S(1)}, u32[]{:S(2)}, u32[]{:S(2)}) collective-permute-start(f32[8,128]{1,0:T(8,128)} %get-tuple-element.23), channel_id=1, source_target_pairs={{0,16},{8,24},{16,0},{24,8},{1,17},{9,25},{17,1},{25,9},{2,18},{10... | collective-permute-start | bytes 12296 | tf_op jit(solution)/shard_map/ppermute | solution.py:317
  29.7 5.6 %collective-permute-start.10 = (f32[8,128]{1,0:T(8,128)}, f32[8,128]{1,0:T(8,128)S(1)}, u32[]{:S(2)}, u32[]{:S(2)}) collective-permute-start(f32[8,128]{1,0:T(8,128)} %get-tuple-element.24), channel_id=1, source_target_pairs={{0,24},{8,16},{16,8},{24,0},{1,25},{9,17},{17,9},{25,1},{2,26},{10... | collective-permute-start | bytes 12296 | tf_op jit(solution)/shard_map/ppermute | solution.py:317
  33.7 1.5 %collective-permute-start.7 = (f32[8,128]{1,0:T(8,128)S(1)}, f32[8,128]{1,0:T(8,128)S(1)}, u32[]{:S(2)}, u32[]{:S(2)}) collective-permute-start(f32[8,128]{1,0:T(8,128)S(1)} %get-tuple-element.21), channel_id=1, source_target_pairs={{0,1},{1,0},{2,3},{3,2},{4,5},{5,4},{6,7},{7,6},{8,9},{9,8},{10,11... | collective-permute-start | bytes 12296 | tf_op jit(solution)/shard_map/ppermute | solution.py:320
  35.3 0.7 %copy-start.3 = (f32[8,128]{1,0:T(8,128)S(1)}, f32[8,128]{1,0:T(8,128)}, u32[]{:S(2)}) copy-start(f32[8,128]{1,0:T(8,128)} %get-tuple-element.15.refs_0_) | copy-start | bytes 12292
where the time goes:
time: 37.1 us; the launch traced here: 36.8 us
  starting transfers between devices  16.4 us (44%)
  Pallas kernels  10.2 us (27%)
  waiting for transfers between devices  6.87 us (19%)
  local copies, waits for them, and re-layouts  2.67 us (7%)
  between operations  0.73 us (2%)
    ppermute x6, starting transfers between devices, to_shard(): return lax.ppermute(array, 'memory', [(i, i ^ step) for i in range(shards)])  11.1 us
    ppermute x6, waiting for transfers between devices, to_shard(): return lax.ppermute(array, 'memory', [(i, i ^ step) for i in range(shards)])  6.85 us
    pallas_call x1, Pallas kernels, score_memory(): pl.pallas_call(functools.partial(memory_kernel, shards, slots), in_specs=...  6.01 us
    ppermute x5, starting transfers between devices, to_group(): return lax.ppermute(array, 'group', [(i, i ^ step) for i in range(groups)])  5.22 us
    unnamed x20, local copies, waits for them, and re-layouts  2.67 us
    pallas_call x1, Pallas kernels, score_batch(): pl.pallas_call(functools.partial(batch_kernel, chips), out_shape=[jax.Sha...  2.44 us
    pallas_call x1, Pallas kernels, pack(): pl.pallas_call(functools.partial(pack_kernel, p_count), in_specs=[vmem, v...  0.91 us
    pallas_call x1, Pallas kernels, finish(): pl.pallas_call(functools.partial(loss_kernel, len(memory_parts)), out_sha...  0.8 us
  transfers between devices with their start and end apart: 11, of which 3 were waited for; matrix products, arithmetic and copies ran while one was open for 0% of the time, Pallas kernels for 23%

commit v1 on v0

--- a/solution.py
+++ b/solution.py
@@ -84,7 +84,7 @@
         functools.partial(pack_kernel, p_count),
         in_specs=[vmem, vmem, pl.BlockSpec(memory_space=pltpu.SMEM)],
         out_shape=jax.ShapeDtypeStruct((1, q_count + 1, q_tokens, depth), queries.dtype),
-        compiler_params=pltpu.CompilerParams(vmem_limit_bytes=4 * MIB),
+        compiler_params=pltpu.CompilerParams(vmem_limit_bytes=56 * MIB),
         name="pack",
     )(queries, candidates, counts)
 
@@ -205,7 +205,7 @@
             pltpu.SemaphoreType.DMA((p_count // CHUNK,)),
             pltpu.SemaphoreType.DMA,
         ],
-        compiler_params=pltpu.CompilerParams(vmem_limit_bytes=57 * MIB),
+        compiler_params=pltpu.CompilerParams(vmem_limit_bytes=52 * MIB),
         cost_estimate=pl.CostEstimate(
             flops=2 * SLOTS * q_tokens * p_count * p_tokens * depth,
             bytes_accessed=2 * p_count * p_tokens * depth,
@@ -321,13 +321,10 @@
 
     own = pack(queries, candidates, counts, memory.shape[1])
     packed = [own] + [to_shard(own, step) for step in range(1, shards)]
-    early, _ = lax.optimization_barrier((positives, own))
-    late, late_queries, _ = lax.optimization_barrier((positives, queries, packed[1]))
-    row = [positives]
-    for step in range(1, chips):
-        near = step & (step - 1) == 0
-        row.append(to_group(early if near else late, 2 * step))
-    mate_queries = to_group(late_queries, 1)
+    sent_positives, _ = lax.optimization_barrier((positives, packed[1]))
+    sent_queries, _ = lax.optimization_barrier((queries, packed[-1]))
+    row = [positives] + [to_group(sent_positives, 2 * step) for step in range(1, chips)]
+    mate_queries = to_group(sent_queries, 1)
 
     scores = score_memory(packed, memory, slots)
     memory_parts = [scores[0]] + [to_shard(scores[step], step) for step in range(1, shards)]

time: 37.1 us -> 34.4 us (0.927)
  waiting for transfers between devices: 6.87 us -> 9.19 us
  Pallas kernels: 10.2 us -> 8.41 us
  local copies, waits for them, and re-layouts: 2.67 us -> 0.9 us
  starting transfers between devices: 16.4 us -> 15 us
    ppermute x6, waiting for transfers between devices: 6.85 us -> 8.88 us  [to_shard(): return lax.ppermute(array, 'memory', [(i, i ^ step) for i in range(shards)])]
    unnamed x20 -> x10, local copies, waits for them, and re-layouts: 2.67 us -> 0.9 us
    ppermute x5, starting transfers between devices: 5.22 us -> 3.49 us  [to_group(): return lax.ppermute(array, 'group', [(i, i ^ step) for i in range(groups)])]
    pallas_call x1, Pallas kernels: 6.01 us -> 4.46 us  [score_memory(): pl.pallas_call(functools.partial(memory_kernel, shards, slots), in_specs=...]
    pallas_call x1, Pallas kernels: 2.44 us -> 1.6 us  [score_batch(): pl.pallas_call(functools.partial(batch_kernel, chips), out_shape=[jax.Sha...]
    pallas_call x1, Pallas kernels: 0.91 us -> 1.54 us  [pack(): pl.pallas_call(functools.partial(pack_kernel, p_count), in_specs=[vmem, v...]
    ppermute x6, starting transfers between devices: 11.1 us -> 11.5 us  [to_shard(): return lax.ppermute(array, 'memory', [(i, i ^ step) for i in range(shards)])]
  transfers between devices with their start and end apart: 11 -> 11, of which waited for: 3 -> 5; matrix products, arithmetic and copies ran while one was open for 0% -> 0% of each run, Pallas kernels for 23% -> 18%
where the time goes in v1:
time: 34.4 us; the launch traced here: 34.2 us
  starting transfers between devices  15 us (44%)
  waiting for transfers between devices  9.19 us (27%)
  Pallas kernels  8.41 us (24%)
  local copies, waits for them, and re-layouts  0.9 us (3%)
  between operations  0.71 us (2%)
    ppermute x6, starting transfers between devices, to_shard(): return lax.ppermute(array, 'memory', [(i, i ^ step) for i in range(shards)])  11.5 us
    ppermute x6, waiting for transfers between devices, to_shard(): return lax.ppermute(array, 'memory', [(i, i ^ step) for i in range(shards)])  8.88 us
    pallas_call x1, Pallas kernels, score_memory(): pl.pallas_call(functools.partial(memory_kernel, shards, slots), in_specs=...  4.46 us
    ppermute x5, starting transfers between devices, to_group(): return lax.ppermute(array, 'group', [(i, i ^ step) for i in range(groups)])  3.49 us
    pallas_call x1, Pallas kernels, score_batch(): pl.pallas_call(functools.partial(batch_kernel, chips), out_shape=[jax.Sha...  1.6 us
    pallas_call x1, Pallas kernels, pack(): pl.pallas_call(functools.partial(pack_kernel, p_count), in_specs=[vmem, v...  1.54 us
    unnamed x10, local copies, waits for them, and re-layouts  0.9 us
    pallas_call x1, Pallas kernels, finish(): pl.pallas_call(functools.partial(loss_kernel, len(memory_parts)), out_sha...  0.8 us
  transfers between devices with their start and end apart: 11, of which 5 were waited for; matrix products, arithmetic and copies ran while one was open for 0% of the time, Pallas kernels for 18%

profile of v1, /device:TPU:0, one launch (start us, length us, event | category | flops | bytes accessed | tf_op | source)
XLA Modules:
  0.0 34.2 jit_solution(12644992734571815533)
XLA Ops:
  0.6 0.0 copy-start.1
  0.6 0.0 copy-start.3
  0.7 0.0 copy-start.2
  0.7 1.5 %pack.1.refs_0_ = bf16[1,9,32,128]{3,2,1,0:T(8,128)(2,1)} custom-call(bf16[1,8,32,128]{3,2,1,0:T(8,128)(2,1)} %refs_0_, s32[1,8,64]{2,1,0:T(8,128)} %refs_4_.3, s32[1,8]{1,0:T(1,128)} %refs_5_.1), custom_call_target="tpu_custom_call" | custom-call | tf_op jit(solution)/shard_map/pack/pallas_call | solution.py:83
  2.2 3.0 %collective-permute-start.2 = (bf16[1,9,32,128]{3,2,1,0:T(8,128)(2,1)}, bf16[1,9,32,128]{3,2,1,0:T(8,128)(2,1)S(1)}, u32[]{:S(2)}, u32[]{:S(2)}) collective-permute-start(bf16[1,9,32,128]{3,2,1,0:T(8,128)(2,1)} %pack.1.refs_0_), channel_id=1, source_target_pairs={{0,8},{8,0},{16,24},{24,16},{1,9},{9,1},{17,25},{25,17},{2,10},{10... | collective-permute-start | bytes 221192 | tf_op jit(solution)/shard_map/ppermute | solution.py:317
  5.2 2.5 %collective-permute-done.2.refs_1_ = bf16[1,9,32,128]{3,2,1,0:T(8,128)(2,1)S(1)} collective-permute-done((bf16[1,9,32,128]{3,2,1,0:T(8,128)(2,1)}, bf16[1,9,32,128]{3,2,1,0:T(8,128)(2,1)S(1)}, u32[]{:S(2)}, u32[]{:S(2)}) %collective-permute-start.2) | collective-permute-done | bytes 73760 | tf_op jit(solution)/shard_map/ppermute | solution.py:317
  7.8 2.9 %collective-permute-start.6 = (bf16[1,8,128,128]{3,2,1,0:T(8,128)(2,1)}, bf16[1,8,128,128]{3,2,1,0:T(8,128)(2,1)S(1)}, u32[]{:S(2)}, u32[]{:S(2)}) collective-permute-start(bf16[1,8,128,128]{3,2,1,0:T(8,128)(2,1)} %refs_2_.1), channel_id=1, source_target_pairs={{0,6},{1,7},{2,4},{3,5},{4,2},{5,3},{6,0},{7,1},{8,14},{9,15},{10,... | collective-permute-start | bytes 786440 | tf_op jit(solution)/shard_map/ppermute | solution.py:320
  10.7 0.5 %collective-permute-start.5 = (bf16[1,8,128,128]{3,2,1,0:T(8,128)(2,1)}, bf16[1,8,128,128]{3,2,1,0:T(8,128)(2,1)S(1)}, u32[]{:S(2)}, u32[]{:S(2)}) collective-permute-start(bf16[1,8,128,128]{3,2,1,0:T(8,128)(2,1)} %refs_2_.1), channel_id=1, source_target_pairs={{0,4},{1,5},{2,6},{3,7},{4,0},{5,1},{6,2},{7,3},{8,12},{9,13},{10,... | collective-permute-start | bytes 786440 | tf_op jit(solution)/shard_map/ppermute | solution.py:320
  11.2 0.1 collective-permute-start.4
  11.3 4.0 %collective-permute-start = (bf16[1,9,32,128]{3,2,1,0:T(8,128)(2,1)}, bf16[1,9,32,128]{3,2,1,0:T(8,128)(2,1)S(1)}, u32[]{:S(2)}, u32[]{:S(2)}) collective-permute-start(bf16[1,9,32,128]{3,2,1,0:T(8,128)(2,1)} %pack.1.refs_0_), channel_id=1, source_target_pairs={{0,24},{8,16},{16,8},{24,0},{1,25},{9,17},{17,9},{25,1},{2,26},{10... | collective-permute-start | bytes 221192 | tf_op jit(solution)/shard_map/ppermute | solution.py:317
  15.3 0.0 collective-permute-start.3
  15.3 2.6 %collective-permute-done.refs_3_ = bf16[1,9,32,128]{3,2,1,0:T(8,128)(2,1)S(1)} collective-permute-done((bf16[1,9,32,128]{3,2,1,0:T(8,128)(2,1)}, bf16[1,9,32,128]{3,2,1,0:T(8,128)(2,1)S(1)}, u32[]{:S(2)}, u32[]{:S(2)}) %collective-permute-start) | collective-permute-done | bytes 73760 | tf_op jit(solution)/shard_map/ppermute | solution.py:317
  17.9 0.0 collective-permute-start.1
  18.0 2.8 %collective-permute-done.3.refs_2_ = bf16[1,9,32,128]{3,2,1,0:T(8,128)(2,1)S(1)} collective-permute-done((bf16[1,9,32,128]{3,2,1,0:T(8,128)(2,1)}, bf16[1,9,32,128]{3,2,1,0:T(8,128)(2,1)S(1)}, u32[]{:S(2)}, u32[]{:S(2)}) %collective-permute-start.3) | collective-permute-done | bytes 73760 | tf_op jit(solution)/shard_map/ppermute | solution.py:317
  20.8 0.9 %copy-done = bf16[1,9,32,128]{3,2,1,0:T(8,128)(2,1)S(1)} copy-done((bf16[1,9,32,128]{3,2,1,0:T(8,128)(2,1)S(1)}, bf16[1,9,32,128]{3,2,1,0:T(8,128)(2,1)}, u32[]{:S(2)}) %copy-start) | copy-done | bytes 73752
  21.7 4.5 %score_memory.1 = (f32[8,128]{1,0:T(8,128)S(1)}, f32[8,128]{1,0:T(8,128)S(1)}, f32[8,128]{1,0:T(8,128)S(1)}, f32[8,128]{1,0:T(8,128)S(1)}) custom-call(bf16[1,9,32,128]{3,2,1,0:T(8,128)(2,1)S(1)} %copy-done, bf16[1,9,32,128]{3,2,1,0:T(8,128)(2,1)S(1)} %collective-permute-done.2.refs_1_, bf16[1,9,32,128]{3,2,1,0:T(8,128)(2,1)S(1)} %collective-permute-done.3.refs_2_, ...), custom_call_target="tpu_custom_call" | custom-call | flops 1073741824 | bytes 4194304 | tf_op jit(solution)/shard_map/score_memory/pallas_call | solution.py:193
  26.1 0.1 collective-permute-start.8
  26.2 0.0 collective-permute-done.1.refs_1_
  26.2 1.5 %collective-permute-start.9 = (f32[8,128]{1,0:T(8,128)S(1)}, f32[8,128]{1,0:T(8,128)S(1)}, u32[]{:S(2)}, u32[]{:S(2)}) collective-permute-start(f32[8,128]{1,0:T(8,128)S(1)} %get-tuple-element.21), channel_id=1, source_target_pairs={{0,16},{8,24},{16,0},{24,8},{1,17},{9,25},{17,1},{25,9},{2,18},{10... | collective-permute-start | bytes 12296 | tf_op jit(solution)/shard_map/ppermute | solution.py:317
  27.7 0.0 collective-permute-done.6.refs_5_
  27.7 2.9 %collective-permute-start.10 = (f32[8,128]{1,0:T(8,128)S(1)}, f32[8,128]{1,0:T(8,128)S(1)}, u32[]{:S(2)}, u32[]{:S(2)}) collective-permute-start(f32[8,128]{1,0:T(8,128)S(1)} %get-tuple-element.22), channel_id=1, source_target_pairs={{0,24},{8,16},{16,8},{24,0},{1,25},{9,17},{17,9},{25,1},{2,26},{10... | collective-permute-start | bytes 12296 | tf_op jit(solution)/shard_map/ppermute | solution.py:317
  30.6 0.0 collective-permute-done.5.refs_4_
  30.6 0.0 collective-permute-done.4.refs_3_
  30.6 0.0 copy-done.1
  30.6 1.6 %score_batch.1 = (f32[8,128]{1,0:T(8,128)S(1)}, f32[8,128]{1,0:T(8,128)S(1)}) custom-call(bf16[1,8,32,128]{3,2,1,0:T(8,128)(2,1)S(1)} %copy-done.1, bf16[1,8,32,128]{3,2,1,0:T(8,128)(2,1)S(1)} %collective-permute-done.1.refs_1_, bf16[1,8,128,128]{3,2,1,0:T(8,128)(2,1)S(1)} %copy-done.4, bf16[1,8,128,128]{3,2,1,0:T(8,128)(2,1)S(1)} %collective-permute-done.4.refs_3_, ...), custom_call_target="tpu_custom_call" | custom-call | flops 536870912 | bytes 1048576 | tf_op jit(solution)/shard_map/score_batch/pallas_call | solution.py:237
  32.2 0.0 collective-permute-start.7
  32.2 0.0 collective-permute-done.8.refs_1_
  32.2 0.0 collective-permute-done.9.refs_2_
  32.3 0.9 %collective-permute-done.10.refs_3_ = f32[8,128]{1,0:T(8,128)S(1)} collective-permute-done((f32[8,128]{1,0:T(8,128)S(1)}, f32[8,128]{1,0:T(8,128)S(1)}, u32[]{:S(2)}, u32[]{:S(2)}) %collective-permute-start.10) | collective-permute-done | bytes 4128 | tf_op jit(solution)/shard_map/ppermute | solution.py:317
  33.1 0.3 collective-permute-done.7.mate_batch
  33.4 0.0 copy-done.2
  33.4 0.8 %finish.1 = (f32[1,8,64]{2,1,0:T(8,128)}, f32[1,8,64]{2,1,0:T(8,128)}, f32[1,8]{1,0:T(1,128)}) custom-call(f32[8,128]{1,0:T(8,128)S(1)} %get-tuple-element.18.own_batch, f32[8,128]{1,0:T(8,128)S(1)} %collective-permute-done.7.mate_batch, f32[8,128]{1,0:T(8,128)S(1)} %get-tuple-element.14.refs_0_, f32[8,128]{1,0:T(8,128)S(1)} %collective-permute-done.8.refs_1_, ...), custom_call_target="tpu_custom_call" | custom-call | tf_op jit(solution)/shard_map/finish/pallas_call | solution.py:297
  (4 shorter events, 0.0 us)
Async XLA Ops:
  0.6 30.0 %copy-start.1 = (bf16[1,8,32,128]{3,2,1,0:T(8,128)(2,1)S(1)}, bf16[1,8,32,128]{3,2,1,0:T(8,128)(2,1)}, u32[]{:S(2)}) copy-start(bf16[1,8,32,128]{3,2,1,0:T(8,128)(2,1)} %refs_0_) | copy-start | bytes 196612
  0.6 32.8 %copy-start.3 = (s32[1,8]{1,0:T(1,128)S(1)}, s32[1,8]{1,0:T(1,128)}, u32[]{:S(2)}) copy-start(s32[1,8]{1,0:T(1,128)} %refs_5_.1) | copy-start | bytes 100
  0.7 32.8 %copy-start.2 = (s32[1,8,64]{2,1,0:T(8,128)S(1)}, s32[1,8,64]{2,1,0:T(8,128)}, u32[]{:S(2)}) copy-start(s32[1,8,64]{2,1,0:T(8,128)} %refs_4_.3) | copy-start | bytes 6148
  2.2 5.6 %collective-permute-start.2 = (bf16[1,9,32,128]{3,2,1,0:T(8,128)(2,1)}, bf16[1,9,32,128]{3,2,1,0:T(8,128)(2,1)S(1)}, u32[]{:S(2)}, u32[]{:S(2)}) collective-permute-start(bf16[1,9,32,128]{3,2,1,0:T(8,128)(2,1)} %pack.1.refs_0_), channel_id=1, source_target_pairs={{0,8},{8,0},{16,24},{24,16},{1,9},{9,1},{17,25},{25,17},{2,10},{10... | collective-permute-start | bytes 221192 | tf_op jit(solution)/shard_map/ppermute | solution.py:317
  7.8 19.9 %collective-permute-start.6 = (bf16[1,8,128,128]{3,2,1,0:T(8,128)(2,1)}, bf16[1,8,128,128]{3,2,1,0:T(8,128)(2,1)S(1)}, u32[]{:S(2)}, u32[]{:S(2)}) collective-permute-start(bf16[1,8,128,128]{3,2,1,0:T(8,128)(2,1)} %refs_2_.1), channel_id=1, source_target_pairs={{0,6},{1,7},{2,4},{3,5},{4,2},{5,3},{6,0},{7,1},{8,14},{9,15},{10,... | collective-permute-start | bytes 786440 | tf_op jit(solution)/shard_map/ppermute | solution.py:320
  10.7 19.9 %collective-permute-start.5 = (bf16[1,8,128,128]{3,2,1,0:T(8,128)(2,1)}, bf16[1,8,128,128]{3,2,1,0:T(8,128)(2,1)S(1)}, u32[]{:S(2)}, u32[]{:S(2)}) collective-permute-start(bf16[1,8,128,128]{3,2,1,0:T(8,128)(2,1)} %refs_2_.1), channel_id=1, source_target_pairs={{0,4},{1,5},{2,6},{3,7},{4,0},{5,1},{6,2},{7,3},{8,12},{9,13},{10,... | collective-permute-start | bytes 786440 | tf_op jit(solution)/shard_map/ppermute | solution.py:320
  11.2 19.4 %collective-permute-start.4 = (bf16[1,8,128,128]{3,2,1,0:T(8,128)(2,1)}, bf16[1,8,128,128]{3,2,1,0:T(8,128)(2,1)S(1)}, u32[]{:S(2)}, u32[]{:S(2)}) collective-permute-start(bf16[1,8,128,128]{3,2,1,0:T(8,128)(2,1)} %refs_2_.1), channel_id=1, source_target_pairs={{0,2},{1,3},{2,0},{3,1},{4,6},{5,7},{6,4},{7,5},{8,10},{9,11},{10,... | collective-permute-start | bytes 786440 | tf_op jit(solution)/shard_map/ppermute | solution.py:320
  11.3 6.7 %collective-permute-start = (bf16[1,9,32,128]{3,2,1,0:T(8,128)(2,1)}, bf16[1,9,32,128]{3,2,1,0:T(8,128)(2,1)S(1)}, u32[]{:S(2)}, u32[]{:S(2)}) collective-permute-start(bf16[1,9,32,128]{3,2,1,0:T(8,128)(2,1)} %pack.1.refs_0_), channel_id=1, source_target_pairs={{0,24},{8,16},{16,8},{24,0},{1,25},{9,17},{17,9},{25,1},{2,26},{10... | collective-permute-start | bytes 221192 | tf_op jit(solution)/shard_map/ppermute | solution.py:317
  15.3 5.5 %collective-permute-start.3 = (bf16[1,9,32,128]{3,2,1,0:T(8,128)(2,1)}, bf16[1,9,32,128]{3,2,1,0:T(8,128)(2,1)S(1)}, u32[]{:S(2)}, u32[]{:S(2)}) collective-permute-start(bf16[1,9,32,128]{3,2,1,0:T(8,128)(2,1)} %pack.1.refs_0_), channel_id=1, source_target_pairs={{0,16},{8,24},{16,0},{24,8},{1,17},{9,25},{17,1},{25,9},{2,18},{10... | collective-permute-start | bytes 221192 | tf_op jit(solution)/shard_map/ppermute | solution.py:317
  17.9 8.3 %collective-permute-start.1 = (bf16[1,8,32,128]{3,2,1,0:T(8,128)(2,1)}, bf16[1,8,32,128]{3,2,1,0:T(8,128)(2,1)S(1)}, u32[]{:S(2)}, u32[]{:S(2)}) collective-permute-start(bf16[1,8,32,128]{3,2,1,0:T(8,128)(2,1)} %refs_0_), channel_id=1, source_target_pairs={{0,1},{1,0},{2,3},{3,2},{4,5},{5,4},{6,7},{7,6},{8,9},{9,8},{10,11... | collective-permute-start | bytes 196616 | tf_op jit(solution)/shard_map/ppermute | solution.py:320
  20.8 0.9 %copy-start = (bf16[1,9,32,128]{3,2,1,0:T(8,128)(2,1)S(1)}, bf16[1,9,32,128]{3,2,1,0:T(8,128)(2,1)}, u32[]{:S(2)}) copy-start(bf16[1,9,32,128]{3,2,1,0:T(8,128)(2,1)} %pack.1.refs_0_) | copy-start | bytes 221188
  21.7 8.9 %copy-start.4 = (bf16[1,8,128,128]{3,2,1,0:T(8,128)(2,1)S(1)}, bf16[1,8,128,128]{3,2,1,0:T(8,128)(2,1)}, u32[]{:S(2)}) copy-start(bf16[1,8,128,128]{3,2,1,0:T(8,128)(2,1)} %refs_2_.1) | copy-start | bytes 786436
  26.1 6.1 %collective-permute-start.8 = (f32[8,128]{1,0:T(8,128)S(1)}, f32[8,128]{1,0:T(8,128)S(1)}, u32[]{:S(2)}, u32[]{:S(2)}) collective-permute-start(f32[8,128]{1,0:T(8,128)S(1)} %get-tuple-element.20), channel_id=1, source_target_pairs={{0,8},{8,0},{16,24},{24,16},{1,9},{9,1},{17,25},{25,17},{2,10},{10... | collective-permute-start | bytes 12296 | tf_op jit(solution)/shard_map/ppermute | solution.py:317
  26.2 6.0 %collective-permute-start.9 = (f32[8,128]{1,0:T(8,128)S(1)}, f32[8,128]{1,0:T(8,128)S(1)}, u32[]{:S(2)}, u32[]{:S(2)}) collective-permute-start(f32[8,128]{1,0:T(8,128)S(1)} %get-tuple-element.21), channel_id=1, source_target_pairs={{0,16},{8,24},{16,0},{24,8},{1,17},{9,25},{17,1},{25,9},{2,18},{10... | collective-permute-start | bytes 12296 | tf_op jit(solution)/shard_map/ppermute | solution.py:317
  27.7 5.4 %collective-permute-start.10 = (f32[8,128]{1,0:T(8,128)S(1)}, f32[8,128]{1,0:T(8,128)S(1)}, u32[]{:S(2)}, u32[]{:S(2)}) collective-permute-start(f32[8,128]{1,0:T(8,128)S(1)} %get-tuple-element.22), channel_id=1, source_target_pairs={{0,24},{8,16},{16,8},{24,0},{1,25},{9,17},{17,9},{25,1},{2,26},{10... | collective-permute-start | bytes 12296 | tf_op jit(solution)/shard_map/ppermute | solution.py:317
  32.2 1.2 %collective-permute-start.7 = (f32[8,128]{1,0:T(8,128)S(1)}, f32[8,128]{1,0:T(8,128)S(1)}, u32[]{:S(2)}, u32[]{:S(2)}) collective-permute-start(f32[8,128]{1,0:T(8,128)S(1)} %get-tuple-element.19), channel_id=1, source_target_pairs={{0,1},{1,0},{2,3},{3,2},{4,5},{5,4},{6,7},{7,6},{8,9},{9,8},{10,11... | collective-permute-start | bytes 12296 | tf_op jit(solution)/shard_map/ppermute | solution.py:320
